TPU v7x, 32 devices: a whole 2x2x4 slice. The times are simulated.
32 devices in a mesh: dp: 4 (over z), expert: 8 (over y, x, core).
Axes of the slice: x: 2, y: 2, z: 4, core: 2. Of those that a mesh axis runs over, the one named last changes fastest.
Arguments:
- tokens: bfloat16 [5120, 2048], P(('dp', 'expert')), may hold values from -6 to 6
- target: bfloat16 [5120, 2048], P(('dp', 'expert')), may hold values from -6 to 6
- expert_ids: int32 [5120, 4], P(('dp', 'expert')), may hold values from 0 to 15, all different within a row; in each aligned block of 160 rows (0 to 159, 160 to 319, ...) at most 60 rows name the same one
- gates: float32 [5120, 4], P(('dp', 'expert')), may hold values from 0.05 to 0.5
- w_in: bfloat16 [2048, 16, 1536], P(None, 'expert'), may hold values from -0.125 to 0.125
- w_out: bfloat16 [768, 16, 2048], P(None, 'expert'), may hold values from -0.21875 to 0.21875
Outputs:
- grad_tokens: bfloat16 [5120, 2048], P(('dp', 'expert'))
- grad_in: bfloat16 [2048, 16, 1536], P('dp', 'expert')
- grad_out: bfloat16 [768, 16, 2048], P(None, 'expert', 'dp')
Inputs may be any that keep to these rules, and one draw needn't show every extreme that they name: `expert_ids`: each token names 4 different experts; in each aligned block of 160 rows (the tokens of one device) no expert is named by more than 60 rows, a bound that some block reaches.
All inputs are finite; a program needn't handle non-finite values.
Results may differ from a plain program's by a relative error of at most 0.012.
Values may be sent and summed in bfloat16 or wider, within the bound.
A program may use at most 192 MiB of HBM per device.

v0:
```python
import jax
import jax.numpy as jnp
from jax import lax
from jax.sharding import PartitionSpec as P


def swiglu_forward(preact, hidden):
    gate_part = preact[..., :hidden]
    up_part = preact[..., hidden:]
    return gate_part * jax.nn.sigmoid(gate_part) * up_part


def swiglu_backward(preact, upstream, hidden):
    gate_part = preact[..., :hidden]
    up_part = preact[..., hidden:]
    sigmoid_value = jax.nn.sigmoid(gate_part)
    silu_value = gate_part * sigmoid_value
    derivative = sigmoid_value * (1.0 + gate_part * (1.0 - sigmoid_value))
    return jnp.concatenate([upstream * up_part * derivative, upstream * silu_value], axis=-1)


def per_device(tokens, target, expert_ids, gates, w_in, w_out):
    tok_rows, model_width = tokens.shape
    route_count = expert_ids.shape[1]
    hidden = w_out.shape[0]
    local_experts = w_in.shape[1]
    expert_peers = lax.axis_size("expert")
    experts_all = local_experts * expert_peers
    capacity = 3 * tok_rows * route_count // (2 * experts_all)
    routes = tok_rows * route_count
    flat_ids = expert_ids.reshape(routes)
    matches = (flat_ids[:, None] == jnp.arange(experts_all, dtype=jnp.int32)[None, :]).astype(
        jnp.int32
    )
    ranking = jnp.sum((jnp.cumsum(matches, axis=0) - 1) * matches, axis=1)
    slot_index = flat_ids * capacity + ranking
    weights_flat = gates.reshape(routes, 1)

    def dispatch(route_rows):
        buffer = (
            jnp.zeros((experts_all * capacity, model_width), route_rows.dtype)
            .at[slot_index]
            .set(route_rows)
        )
        return buffer.reshape(expert_peers, local_experts, capacity, model_width)

    sent_rows = lax.all_to_all(
        dispatch(jnp.repeat(tokens, route_count, axis=0)),
        "expert",
        split_axis=0,
        concat_axis=0,
        tiled=True,
    )
    preact = jnp.einsum("sekd,deh->sekh", sent_rows, w_in, preferred_element_type=jnp.float32)
    activation = swiglu_forward(preact, hidden).astype(jnp.bfloat16)
    outputs = jnp.einsum(
        "sekh,hed->sekd", activation, w_out, preferred_element_type=jnp.float32
    ).astype(jnp.bfloat16)
    returned = lax.all_to_all(outputs, "expert", split_axis=0, concat_axis=0, tiled=True)
    route_rows = returned.reshape(experts_all * capacity, model_width)[slot_index]
    student = tokens.astype(jnp.float32) + jnp.sum(
        route_rows.astype(jnp.float32).reshape(tok_rows, route_count, model_width)
        * weights_flat.reshape(tok_rows, route_count, 1),
        axis=1,
    )
    residual_grad = student - target.astype(jnp.float32)
    scaled = (weights_flat * jnp.repeat(residual_grad, route_count, axis=0)).astype(jnp.bfloat16)
    sent_grads = lax.all_to_all(dispatch(scaled), "expert", split_axis=0, concat_axis=0, tiled=True)
    act_grad = jnp.einsum("sekd,hed->sekh", sent_grads, w_out, preferred_element_type=jnp.float32)
    pre_grad = swiglu_backward(preact, act_grad, hidden).astype(jnp.bfloat16)
    input_grads = jnp.einsum(
        "sekh,deh->sekd", pre_grad, w_in, preferred_element_type=jnp.float32
    ).astype(jnp.bfloat16)
    returned_grads = lax.all_to_all(input_grads, "expert", split_axis=0, concat_axis=0, tiled=True)
    route_back = returned_grads.reshape(experts_all * capacity, model_width)[slot_index]
    grad_tokens = (
        residual_grad
        + jnp.sum(
            route_back.astype(jnp.float32).reshape(tok_rows, route_count, model_width), axis=1
        )
    ).astype(jnp.bfloat16)
    term_in = jnp.einsum("sekd,sekh->deh", sent_rows, pre_grad, preferred_element_type=jnp.float32)
    term_out = jnp.einsum(
        "sekh,sekd->hed", activation, sent_grads, preferred_element_type=jnp.float32
    )
    grad_in, grad_out = (
        lax.psum_scatter(
            term_in.astype(jnp.bfloat16), "dp", scatter_dimension=0, tiled=True
        ).astype(jnp.float32),
        lax.psum_scatter(
            term_out.astype(jnp.bfloat16), "dp", scatter_dimension=2, tiled=True
        ).astype(jnp.float32),
    )
    return (grad_tokens, grad_in.astype(jnp.bfloat16), grad_out.astype(jnp.bfloat16))


def solution(mesh):
    in_specs = (
        P(("dp", "expert"), None),
        P(("dp", "expert"), None),
        P(("dp", "expert"), None),
        P(("dp", "expert"), None),
        P(None, "expert", None),
        P(None, "expert", None),
    )
    out_specs = (P(("dp", "expert"), None), P("dp", "expert", None), P(None, "expert", "dp"))
    return jax.shard_map(
        per_device, mesh=mesh, in_specs=in_specs, out_specs=out_specs, check_vma=False
    )
```

profile of v0, /device:TPU:0, one launch (start us, length us, event | category | flops | bytes accessed | tf_op | source)
XLA Modules:
  0.0 642.5 jit_solution(9860573791525961220)
XLA Ops:
  7.2 0.7 broadcast_multiply_fusion
  7.9 0.8 copy.33
  8.7 0.1 eq.29
  8.8 0.1 eq.25
  8.9 0.1 copy.32
  9.0 0.1 mul.61
  9.1 1.4 reduce-window.6
  10.5 0.2 slice_reduce_fusion
  10.8 2.4 broadcast_in_dim.4
  13.2 2.8 reshape.112
  16.0 0.1 fusion.31
  16.1 10.3 %scatter_custom_fusion = bf16[960,2048]{1,0:T(8,128)(2,1)} fusion(s32[640]{0:T(1024)S(1)} %fusion.33, bf16[640,2048]{1,0:T(8,128)(2,1)} %reshape.112, bf16[]{:T(256)} %constant.7.clone.1), kind=kCustom, calls=%fused_computation.37 | custom fusion | bytes 3932672 | tf_op jit(solution)/shard_map/scatter | solution.py:43
  26.4 4.9 reshape.85
  31.3 6.2 copy.36
  37.5 51.4 %all_to_all.20 = bf16[8,2,60,2048]{3,1,2,0:T(2,128)(2,1)S(1)} all-to-all(bf16[8,2,60,2048]{3,1,2,0:T(2,128)(2,1)S(1)} %copy.36), channel_id=1, replica_groups=mesh['dp'=4,'expert'=8] {'expert'}, dimensions={0} | all-to-all | bytes 7864320 | tf_op jit(solution)/shard_map/all_to_all | solution.py:47
  88.9 13.4 %fusion.10 = f32[8,2,60,1536]{3,2,0,1:T(8,128)S(1)} fusion(bf16[2048,2,1536,1]{2,1,0,3:T(2,128)(2,1)} %bitcast.54, bf16[8,2,60,2048]{3,1,2,0:T(2,128)(2,1)S(1)} %all_to_all.20), kind=kOutput, calls=%fused_computation.18 | convolution fusion | flops 6039797760 | bytes 22413312 | tf_op jit(solution)/shard_map/sekd,deh->sekh/dot_general | solution.py:54
  102.4 0.0 copy-done.1
  102.4 0.0 copy-start
  102.4 1.0 multiply_convert_fusion.1
  103.3 1.7 copy-done
  105.0 1.1 copy-done.5
  106.2 11.2 %convert_bitcast_fusion.1 = bf16[8,2,60,2048]{3,2,0,1:T(8,128)(2,1)S(1)} fusion(bf16[8,2,60,768]{3,2,0,1:T(8,128)(2,1)S(1)} %multiply_convert_fusion.1, bf16[768,2,2048,1]{2,1,0,3:T(2,128)(2,1)} %bitcast.56), kind=kOutput, calls=%fused_computation.20 | convolution fusion | flops 3021864960 | bytes 11698176 | tf_op jit(solution)/shard_map/sekh,hed->sekd/dot_general | solution.py:56
  117.4 6.0 copy.40
  123.4 4.7 all-to-all-start.1
  128.1 0.0 reduce-scatter.5.cloned.1.call-start
  128.1 0.0 copy-done.8
  128.1 0.1 copy.42
  128.2 0.1 mul.67
  128.4 46.0 %all-to-all-done.1 = bf16[8,2,60,2048]{3,1,2,0:T(2,128)(2,1)} async-done(((bf16[8,2,60,2048]{3,1,2,0:T(2,128)(2,1)}), bf16[8,2,60,2048]{3,1,2,0:T(2,128)(2,1)}, u32[]{:S(2)}, u32[]{:S(2)}) %all-to-all-start.1) | async-done | bytes 3932192 | tf_op jit(solution)/shard_map/all_to_all | solution.py:59
  174.4 6.0 copy.41
  180.4 5.1 reshape.86
  185.4 9.0 %gather_fusion = bf16[640,2048]{1,0:T(8,128)(2,1)S(1)} fusion(bf16[960,2048]{1,0:T(8,128)(2,1)} %reshape.86, s32[1024]{0:T(1024)S(1)} %pad_clamp_fusion), kind=kCustom, calls=%fused_computation | custom fusion | bytes 5245440 | tf_op jit(solution)/shard_map/gather | solution.py:60
  194.4 4.1 reshape.90
  198.5 6.7 %multiply_reduce_fusion = f32[160,2048]{1,0:T(8,128)S(1)} fusion(f32[160,4,2048]{2,1,0:T(4,128)} %reshape.90, f32[160,4]{1,0:T(8,128)S(1)} %copy.42), kind=kLoop, calls=%fused_computation.17 | loop fusion | flops 2293760 | bytes 6556160 | tf_op jit(solution)/shard_map/reduce_sum | solution.py:61
  205.2 0.0 copy-done.4
  205.2 0.0 copy-done.7
  205.2 0.3 convert_subtract_fusion
  205.5 3.8 broadcast_in_dim.5
  209.2 7.3 %reshape.87 = f32[640,2048]{1,0:T(8,128)} reshape(f32[160,4,2048]{2,1,0:T(4,128)} %broadcast_in_dim.5) | data formatting | bytes 10485760 | tf_op jit(solution)/shard_map/reshape | solution.py:67
  216.5 14.8 %scatter_custom_fusion.1 = bf16[960,2048]{1,0:T(8,128)(2,1)} fusion(s32[640]{0:T(1024)S(1)} %fusion.33, f32[640,2048]{1,0:T(8,128)} %reshape.87, f32[640]{0:T(1024)S(1)} %mul.67, bf16[]{:T(256)} %constant.7.clone.1), kind=kCustom, calls=%fused_computation.34 | custom fusion | flops 2621440 | bytes 9179138 | tf_op jit(solution)/shard_map/scatter | solution.py:43
  231.3 4.9 reshape.88
  236.2 6.2 copy.44
  242.5 0.0 copy-start.6
  242.5 49.1 %all_to_all.21 = bf16[8,2,60,2048]{3,1,2,0:T(2,128)(2,1)S(1)} all-to-all(bf16[8,2,60,2048]{3,1,2,0:T(2,128)(2,1)S(1)} %copy.44), channel_id=1, replica_groups=mesh['dp'=4,'expert'=8] {'expert'}, dimensions={0} | all-to-all | bytes 7864320 | tf_op jit(solution)/shard_map/all_to_all | solution.py:68
  291.5 1.9 copy-done.3
  293.5 7.9 %fusion.5 = bf16[768,2,2048]{0,2,1:T(8,128)(2,1)} fusion(bf16[8,2,60,768]{3,2,0,1:T(8,128)(2,1)S(1)} %copy-done.6, bf16[8,2,60,2048]{3,1,2,0:T(2,128)(2,1)S(1)} %all_to_all.21), kind=kOutput, calls=%fused_computation.11 | convolution fusion | flops 3023044608 | bytes 11698176 | tf_op jit(solution)/shard_map/sekh,sekd->hed/dot_general | solution.py:83
  301.4 0.0 reduce-scatter.5.cloned.1.call-update
  301.4 0.0 reduce-scatter.3.cloned.1.call-start
  301.5 15.0 %fusion.22 = (bf16[8,2,60,768]{3,2,0,1:T(8,128)(2,1)S(1)}, bf16[8,2,60,768]{3,2,0,1:T(8,128)(2,1)}) fusion(f32[8,2,60,1536]{3,2,0,1:T(8,128)} %copy-done, bf16[768,2,2048,1]{2,1,0,3:T(2,128)(2,1)} %bitcast.57, bf16[8,2,60,2048]{3,1,2,0:T(2,128)(2,1)} %copy-done.3), kind=kOutput, calls=%fused_computation.29 | convolution fusion | flops 3029483520 | bytes 19070976 | tf_op jit(solution)/shard_map/sekd,hed->sekh/dot_general | solution.py:69
  316.5 1.1 copy-done.9
  317.6 11.9 %fusion.4 = bf16[2048,2,1536]{0,2,1:T(8,128)(2,1)} fusion(bf16[8,2,60,2048]{3,1,2,0:T(2,128)(2,1)S(1)} %copy-done.2, bf16[8,2,60,768]{3,2,0,1:T(8,128)(2,1)} %get-tuple-element.13, bf16[8,2,60,768]{3,2,0,1:T(8,128)(2,1)S(1)} %get-tuple-element.12), kind=kOutput, calls=%fused_computation.10 | convolution fusion | flops 6051987456 | bytes 19464192 | tf_op jit(solution)/shard_map/sekd,sekh->deh/dot_general | solution.py:82
  329.6 0.0 reduce-scatter.3.cloned.1.call-update
  329.6 13.5 %convert_bitcast_fusion = bf16[8,2,60,2048]{3,2,0,1:T(8,128)(2,1)} fusion(bf16[2048,2,1536,1]{2,1,0,3:T(2,128)(2,1)} %bitcast.55, bf16[8,2,60,768]{3,2,0,1:T(8,128)(2,1)} %get-tuple-element.13, bf16[8,2,60,768]{3,2,0,1:T(8,128)(2,1)} %copy-done.9), kind=kOutput, calls=%fused_computation.19 | convolution fusion | flops 6047662080 | bytes 19464192 | tf_op jit(solution)/shard_map/sekh,deh->sekd/dot_general | solution.py:71
  343.1 6.2 copy.48
  349.3 49.0 %all_to_all.22 = bf16[8,2,60,2048]{3,1,2,0:T(2,128)(2,1)S(1)} all-to-all(bf16[8,2,60,2048]{3,1,2,0:T(2,128)(2,1)S(1)} %copy.48), channel_id=1, replica_groups=mesh['dp'=4,'expert'=8] {'expert'}, dimensions={0} | all-to-all | bytes 7864320 | tf_op jit(solution)/shard_map/all_to_all | solution.py:74
  398.3 3.9 copy.49
  402.2 5.0 reshape.89
  407.2 9.5 %gather_fusion.1 = bf16[640,2048]{1,0:T(8,128)(2,1)} fusion(bf16[960,2048]{1,0:T(8,128)(2,1)} %reshape.89, s32[1024]{0:T(1024)S(1)} %pad_clamp_fusion), kind=kCustom, calls=%fused_computation.1 | custom fusion | bytes 5245440 | tf_op jit(solution)/shard_map/gather | solution.py:75
  416.7 5.9 reshape.91
  422.7 5.8 reduce_sum.32
  428.5 1.0 add_convert_fusion
  429.5 4.9 copy.53
  434.4 192.1 %reduce-scatter.3.cloned.1.call-done = bf16[512,2,1536]{0,2,1:T(8,128)(2,1)} async-done(((bf16[2048,2,1536]{0,2,1:T(8,128)(2,1)}), bf16[512,2,1536]{0,2,1:T(8,128)(2,1)}) %reduce-scatter.3.cloned.1.call-update) | async-done | bytes 3145744 | tf_op jit(solution)/shard_map/reduce_scatter | solution.py:87
  626.5 8.7 %copy.52 = bf16[512,2,1536]{2,1,0:T(2,128)(2,1)} copy(bf16[512,2,1536]{0,2,1:T(8,128)(2,1)} %reduce-scatter.3.cloned.1.call-done) | data formatting | bytes 6291456
  (15 shorter events, 0.1 us)
Async XLA Ops:
  88.9 13.4 %copy-start.1 = (bf16[8,2,60,2048]{3,1,2,0:T(2,128)(2,1)}, bf16[8,2,60,2048]{3,1,2,0:T(2,128)(2,1)S(1)}, u32[]{:S(2)}) copy-start(bf16[8,2,60,2048]{3,1,2,0:T(2,128)(2,1)S(1)} %all_to_all.20) | copy-start | bytes 11796484
  102.4 2.7 copy-start
  105.0 1.1 copy-start.5
  123.4 4.7 copy-start.8
  123.4 51.0 %all-to-all-start.1 = ((bf16[8,2,60,2048]{3,1,2,0:T(2,128)(2,1)}), bf16[8,2,60,2048]{3,1,2,0:T(2,128)(2,1)}, u32[]{:S(2)}, u32[]{:S(2)}) async-start(bf16[8,2,60,2048]{3,1,2,0:T(2,128)(2,1)} %copy.40), calls=%async_computation.1 | async-start | bytes 7864320 | tf_op jit(solution)/shard_map/all_to_all | solution.py:59
  128.1 301.4 %reduce-scatter.5.cloned.1.call-start = ((), (), s32[]{:S(2)}) async-start(), calls=%async_computation.7 | async-start | bytes 7864320 | tf_op jit(solution)/shard_map/reduce_scatter | solution.py:90
  198.5 6.7 %copy-start.4 = (bf16[160,2048]{1,0:T(8,128)(2,1)S(1)}, bf16[160,2048]{1,0:T(8,128)(2,1)}, u32[]{:S(2)}) copy-start(bf16[160,2048]{1,0:T(8,128)(2,1)} %param.6) | copy-start | bytes 1966084
  198.5 6.7 %copy-start.7 = (bf16[160,2048]{1,0:T(8,128)(2,1)S(1)}, bf16[160,2048]{1,0:T(8,128)(2,1)}, u32[]{:S(2)}) copy-start(bf16[160,2048]{1,0:T(8,128)(2,1)} %param.7) | copy-start | bytes 1966084
  242.5 51.0 %copy-start.6 = (bf16[8,2,60,768]{3,2,0,1:T(8,128)(2,1)S(1)}, bf16[8,2,60,768]{3,2,0,1:T(8,128)(2,1)}, u32[]{:S(2)}) copy-start(bf16[8,2,60,768]{3,2,0,1:T(8,128)(2,1)} %copy-done.5) | copy-start | bytes 4423684
  291.5 1.9 copy-start.3
  301.4 325.0 %reduce-scatter.3.cloned.1.call-start = ((), (), s32[]{:S(2)}) async-start(), calls=%async_computation.6 | async-start | bytes 15728640 | tf_op jit(solution)/shard_map/reduce_scatter | solution.py:87
  301.5 16.1 %copy-start.2 = (bf16[8,2,60,2048]{3,1,2,0:T(2,128)(2,1)S(1)}, bf16[8,2,60,2048]{3,1,2,0:T(2,128)(2,1)}, u32[]{:S(2)}) copy-start(bf16[8,2,60,2048]{3,1,2,0:T(2,128)(2,1)} %copy-done.1) | copy-start | bytes 11796484
  316.5 1.1 copy-start.9
Sparse Core Ops, SparseCore 0:
  301.6 110.1 reduce-scatter.4
  414.1 212.3 reduce-scatter.2
where the time goes:
time: 652 us; the launch traced here: 643 us
  waiting for transfers between devices  238 us (37%)
  blocking collectives  149 us (23%)
  local copies, waits for them, and re-layouts  131 us (20%)
  matrix products  73 us (11%)
  other arithmetic  31.8 us (5%)
  between operations  14.7 us (2%)
    reduce_scatter x1, waiting for transfers between devices, per_device(): lax.psum_scatter(term_in.astype(jnp.bfloat16), 'dp', scatter_dimension=0,...  192 us
    all_to_all x1, blocking collectives, per_device(): lax.all_to_all(dispatch(jnp.repeat(tokens, route_count, axis=0)), 'expert...  51.4 us
    all_to_all x1, blocking collectives, per_device(): lax.all_to_all(dispatch(scaled), 'expert', split_axis=0, concat_axis=0, t...  49.1 us
    all_to_all x1, blocking collectives, per_device(): lax.all_to_all(input_grads, 'expert', split_axis=0, concat_axis=0, tiled=...  49 us
    all_to_all x1, waiting for transfers between devices, per_device(): lax.all_to_all(outputs, 'expert', split_axis=0, concat_axis=0, tiled=True)  46 us
    reshape x4, local copies, waits for them, and re-layouts, dispatch(): return buffer.reshape(expert_peers, local_experts, capacity, model_width)  22.3 us
    unnamed x24, local copies, waits for them, and re-layouts  20.5 us
    dot_general x1, matrix products, per_device(): jnp.einsum('sekd,hed->sekh', sent_grads, w_out, preferred_element_type=jn...  15 us
  transfers between devices with their start and end apart: 3, of which 2 were waited for; matrix products, arithmetic and copies ran while one was open for 13% of the time, Pallas kernels for 0%

commit v1 on v0

v1 whole, which is shorter than its diff:
```python
import jax
import jax.numpy as jnp
from jax import lax
from jax.sharding import PartitionSpec as P


def swiglu_forward(preact, hidden):
    gate_part = preact[..., :hidden]
    up_part = preact[..., hidden:]
    return gate_part * jax.nn.sigmoid(gate_part) * up_part


def swiglu_backward(preact, upstream, hidden):
    gate_part = preact[..., :hidden]
    up_part = preact[..., hidden:]
    sigmoid_value = jax.nn.sigmoid(gate_part)
    silu_value = gate_part * sigmoid_value
    derivative = sigmoid_value * (1.0 + gate_part * (1.0 - sigmoid_value))
    return jnp.concatenate([upstream * up_part * derivative, upstream * silu_value], axis=-1)


def dot32(spec, left, right):
    return jnp.einsum(spec, left, right, preferred_element_type=jnp.float32)


def per_device(tokens, target, expert_ids, gates, w_in, w_out):
    tok_rows, model_width = tokens.shape
    route_count = expert_ids.shape[1]
    hidden = w_out.shape[0]
    local_experts = w_in.shape[1]
    peers = lax.axis_size("expert")
    experts_all = local_experts * peers
    capacity = 3 * tok_rows * route_count // (2 * experts_all)
    slots = -(-capacity // 16) * 16
    rows = peers * slots

    block = lax.all_gather(tokens, "expert")
    ids = lax.all_gather(expert_ids, "expert")
    weights = lax.all_gather(gates, "expert")
    first = lax.axis_index("expert") * local_experts
    picks, slot_gates = [], []
    for e in range(local_experts):
        named = ids == first + e
        member = jnp.any(named, axis=2)
        gate = jnp.sum(jnp.where(named, weights, 0.0), axis=2)
        place = jnp.cumsum(member.astype(jnp.int32), axis=1) - 1
        place = jnp.where(member, place, -1)
        pick = place[:, None, :] == jnp.arange(slots, dtype=jnp.int32)[None, :, None]
        picks.append(pick.astype(jnp.bfloat16))
        slot_gates.append(
            jnp.sum(jnp.where(pick, gate[:, None, :], 0.0), axis=2).reshape(rows, 1)
        )
    pick_all = jnp.concatenate(picks, axis=1)

    def dispatch(e, blocks):
        return dot32("bst,btd->bsd", picks[e], blocks).reshape(rows, model_width)

    def combine(parts):
        stacked = jnp.concatenate(
            [part.reshape(peers, slots, model_width) for part in parts], axis=1
        )
        total = dot32("bst,bsd->btd", pick_all, stacked).astype(jnp.bfloat16)
        return lax.psum_scatter(
            total.reshape(peers * tok_rows, model_width), "expert", scatter_dimension=0, tiled=True
        ).astype(jnp.float32)

    weights_in = [w_in[:, e, :] for e in range(local_experts)]
    weights_out = [w_out[:, e, :] for e in range(local_experts)]

    sent, preacts, activations, outputs = [], [], [], []
    for e in range(local_experts):
        sent.append(dispatch(e, block).astype(jnp.bfloat16))
        preacts.append(dot32("sd,dh->sh", sent[e], weights_in[e]))
        activations.append(swiglu_forward(preacts[e], hidden).astype(jnp.bfloat16))
        outputs.append(
            (dot32("sh,hd->sd", activations[e], weights_out[e]) * slot_gates[e]).astype(
                jnp.bfloat16
            )
        )
    student = tokens.astype(jnp.float32) + combine(outputs)
    residual_grad = student - target.astype(jnp.float32)

    grad_block = lax.all_gather(residual_grad.astype(jnp.bfloat16), "expert")
    input_grads, terms_in, terms_out = [], [], []
    for e in range(local_experts):
        scaled = (dispatch(e, grad_block) * slot_gates[e]).astype(jnp.bfloat16)
        terms_out.append(dot32("sh,sd->hd", activations[e], scaled).astype(jnp.bfloat16))
        act_grad = dot32("sd,hd->sh", scaled, weights_out[e])
        pre_grad = swiglu_backward(preacts[e], act_grad, hidden).astype(jnp.bfloat16)
        terms_in.append(dot32("sd,sh->dh", sent[e], pre_grad).astype(jnp.bfloat16))
        input_grads.append(dot32("sh,dh->sd", pre_grad, weights_in[e]).astype(jnp.bfloat16))
    grad_out = [
        lax.psum_scatter(term, "dp", scatter_dimension=1, tiled=True) for term in terms_out
    ]
    grad_in = [lax.psum_scatter(term, "dp", scatter_dimension=0, tiled=True) for term in terms_in]
    grad_tokens = (residual_grad + combine(input_grads)).astype(jnp.bfloat16)
    return grad_tokens, jnp.stack(grad_in, axis=1), jnp.stack(grad_out, axis=1)


def solution(mesh):
    in_specs = (
        P(("dp", "expert"), None),
        P(("dp", "expert"), None),
        P(("dp", "expert"), None),
        P(("dp", "expert"), None),
        P(None, "expert", None),
        P(None, "expert", None),
    )
    out_specs = (P(("dp", "expert"), None), P("dp", "expert", None), P(None, "expert", "dp"))
    return jax.shard_map(
        per_device, mesh=mesh, in_specs=in_specs, out_specs=out_specs, check_vma=False
    )
```

time: 652 us -> 636 us (0.975)
  waiting for transfers between devices: 238 us -> 447 us
  blocking collectives: 149 us -> 19.6 us
  local copies, waits for them, and re-layouts: 131 us -> 49.5 us
  other arithmetic: 31.8 us -> 12.8 us
  matrix products: 73 us -> 84.9 us
    reduce_scatter x2 -> x6, waiting for transfers between devices: 192 us -> 405 us  [the longest x2 224 us: per_device(): lax.psum_scatter(term, 'dp', scatter_dimension=0, tiled=True)]
    all_to_all x3 -> x0, blocking collectives: 149 us -> none  [the longest x1 51.4 us: per_device(): lax.all_to_all(dispatch(jnp.repeat(tokens, route_count, axis=0)), 'expert...]
    all_to_all x1 -> x0, waiting for transfers between devices: 46 us -> none  [per_device(): lax.all_to_all(outputs, 'expert', split_axis=0, concat_axis=0, tiled=True)]
    reshape x8 -> x0, local copies, waits for them, and re-layouts: 42.3 us -> none  [the longest x4 22.3 us: dispatch(): return buffer.reshape(expert_peers, local_experts, capacity, model_width)]
    all_gather x0 -> x2, waiting for transfers between devices: none -> 41.2 us  [the longest x1 41.2 us: per_device(): grad_block = lax.all_gather(residual_grad.astype(jnp.bfloat16), 'expert')]
    slice x1 -> x3, local copies, waits for them, and re-layouts: 0.25 us -> 35.7 us  [the longest x1 19.3 us: per_device(): weights_in = [w_in[:, e, :] for e in range(local_experts)]]
    convert_element_type x4 -> x0, local copies, waits for them, and re-layouts: 22.2 us -> none  [the longest x1 6.24 us: per_device(): input_grads = jnp.einsum('sekh,deh->sekd', pre_grad, w_in, preferred_elem...]
    all_gather x0 -> x2, blocking collectives: none -> 19.6 us  [the longest x1 10.7 us: per_device(): ids = lax.all_gather(expert_ids, 'expert')]
  transfers between devices with their start and end apart: 3 -> 8, of which waited for: 2 -> 7; matrix products, arithmetic and copies ran while one was open for 13% -> 15% of each run, Pallas kernels for 0% -> 0%
where the time goes in v1:
time: 636 us; the launch traced here: 630 us
  waiting for transfers between devices  447 us (70%)
  matrix products  84.9 us (13%)
  local copies, waits for them, and re-layouts  49.5 us (8%)
  blocking collectives  19.6 us (3%)
  between operations  14.9 us (2%)
  other arithmetic  12.8 us (2%)
    reduce_scatter x2, waiting for transfers between devices, per_device(): lax.psum_scatter(term, 'dp', scatter_dimension=0, tiled=True)  224 us
    reduce_scatter x2, waiting for transfers between devices, combine(): lax.psum_scatter(total.reshape(peers * tok_rows, model_width), 'expert',...  113 us
    dot_general x18, matrix products, dot32(): return jnp.einsum(spec, left, right, preferred_element_type=jnp.float32)  84.9 us
    reduce_scatter x2, waiting for transfers between devices, per_device(): lax.psum_scatter(term, 'dp', scatter_dimension=1, tiled=True)  67.7 us
    all_gather x1, waiting for transfers between devices, per_device(): grad_block = lax.all_gather(residual_grad.astype(jnp.bfloat16), 'expert')  41.2 us
    slice x1, local copies, waits for them, and re-layouts, per_device(): weights_in = [w_in[:, e, :] for e in range(local_experts)]  19.3 us
    slice x1, local copies, waits for them, and re-layouts, per_device(): weights_out = [w_out[:, e, :] for e in range(local_experts)]  16.3 us
    unnamed x68, local copies, waits for them, and re-layouts  13.4 us
  transfers between devices with their start and end apart: 8, of which 7 were waited for; matrix products, arithmetic and copies ran while one was open for 15% of the time, Pallas kernels for 0%

profile of v1, /device:TPU:0, one launch (start us, length us, event | category | flops | bytes accessed | tf_op | source)
XLA Modules:
  0.0 629.6 jit_solution(14339345351211411788)
XLA Ops:
  7.2 0.0 all-gather.9.cloned.1.call-start
  7.2 0.7 all-gather.9.cloned.1.call-update
  7.9 0.0 reduce-scatter.7.cloned.1.call-start
  8.0 10.7 %all-gather.4 = s32[8,160,4]{1,2,0:T(4,128)S(1)} all-gather(s32[1,160,4]{1,2,0:T(4,128)} %bitcast.102), channel_id=2, replica_groups=mesh['dp'=4,'expert'=8] {'expert'}, dimensions={0}, use_global_device_ids=true | all-gather | bytes 23040 | tf_op jit(solution)/shard_map/all_gather | solution.py:38
  18.7 0.6 reduce-window.14
  19.3 0.2 slice_reduce_fusion.1
  19.5 8.9 %all-gather.5 = f32[8,160,4]{1,2,0:T(4,128)S(1)} all-gather(f32[1,160,4]{1,2,0:T(4,128)} %bitcast.103), channel_id=4, replica_groups=mesh['dp'=4,'expert'=8] {'expert'}, dimensions={0}, use_global_device_ids=true | all-gather | bytes 23040 | tf_op jit(solution)/shard_map/all_gather | solution.py:39
  28.4 0.1 select_reduce_fusion.3
  28.5 0.6 reduce-window.16
  29.1 0.2 slice_reduce_fusion
  29.4 0.1 add_bitcast_fusion.1
  29.4 0.1 add_bitcast_fusion
  29.5 0.9 select_reduce_fusion
  30.4 0.1 mul.97
  30.5 0.1 mul.92
  30.6 0.5 iota_compare_fusion
  31.1 16.3 %fusion.39 = (bf16[768,1,2048]{2,1,0:T(2,128)(2,1)}, bf16[768,1,2048]{2,1,0:T(2,128)(2,1)}) fusion(bf16[768,2,2048]{2,1,0:T(2,128)(2,1)} %param.11), kind=kLoop, calls=%fused_computation.84 | loop fusion | bytes 12582912 | tf_op jit(solution)/shard_map/slice | solution.py:68
  47.4 19.3 %fusion.38 = (bf16[2048,1,1536]{2,1,0:T(2,128)(2,1)}, bf16[2048,1,1536]{2,1,0:T(2,128)(2,1)}) fusion(bf16[2048,2,1536]{2,1,0:T(2,128)(2,1)S(1)} %bitcast.71), kind=kLoop, calls=%fused_computation.83 | loop fusion | bytes 25165824 | tf_op jit(solution)/shard_map/slice | solution.py:67
  66.7 4.0 convolution_convert_fusion.6
  70.7 1.4 convolution_convert_fusion.7
  72.2 8.3 %fusion.16 = f32[512,1536]{1,0:T(8,128)S(1)} fusion(bf16[512,2048]{1,0:T(8,128)(2,1)S(1)} %bitcast.94, bf16[2048,1,1536]{2,1,0:T(2,128)(2,1)} %get-tuple-element.17), kind=kOutput, calls=%fused_computation.31 | convolution fusion | flops 3221225472 | bytes 11534336 | tf_op jit(solution)/shard_map/sd,dh->sh/dot_general | solution.py:23
  80.5 1.6 copy-done.2
  82.1 0.5 multiply_convert_fusion.9
  82.7 3.4 fusion.17
  86.1 0.5 multiply_convert_fusion.8
  86.6 2.4 multiply_convert_fusion.3
  89.0 0.4 slice-done.13
  89.4 0.7 slice-done.14
  90.1 2.4 multiply_convert_fusion.2
  92.5 3.3 fusion.13
  95.8 0.0 all-gather.11.cloned.1.call-start
  95.9 56.9 %reduce-scatter.7.cloned.1.call-done = bf16[160,2048]{1,0:T(8,128)(2,1)} async-done(((bf16[1280,2048]{1,0:T(8,128)(2,1)}), bf16[160,2048]{1,0:T(8,128)(2,1)}) %reduce-scatter.7.cloned.1.call-update) | async-done | bytes 655376 | tf_op jit(solution)/shard_map/reduce_scatter | solution.py:63
  152.7 2.2 fusion.22
  155.0 0.3 reduce-scatter.15.cloned.1.call-start
  155.3 41.2 %all-gather.11.cloned.1.call-done = bf16[1280,2048]{1,0:T(8,128)(2,1)} async-done(((bf16[160,2048]{1,0:T(8,128)(2,1)}), bf16[1280,2048]{1,0:T(8,128)(2,1)}) %all-gather.11.cloned.1.call-update) | async-done | bytes 5242896 | tf_op jit(solution)/shard_map/all_gather | solution.py:83
  196.5 5.3 multiply_convert_fusion.1
  201.8 0.3 fusion.9
  202.1 3.5 convolution_convert_fusion.3
  205.6 0.0 reduce-scatter.17.cloned.1.call-start
  205.6 5.3 multiply_convert_fusion
  210.9 0.3 fusion.8
  211.2 3.4 convolution_convert_fusion.2
  214.7 0.4 reduce-scatter.9.cloned.1.call-start
  215.2 8.6 %multiply_convert_fusion.5 = (bf16[512,768]{1,0:T(8,128)(2,1)}, bf16[512,768]{1,0:T(8,128)(2,1)}) fusion(f32[512,1536]{1,0:T(8,128)} %copy-done.4, bf16[512,2048]{1,0:T(8,128)(2,1)} %bitcast.97, bf16[768,1,2048]{2,1,0:T(2,128)(2,1)} %get-tuple-element.20), kind=kOutput, calls=%fused_computation.37 | convolution fusion | flops 1615724544 | bytes 9961472 | tf_op jit(solution)/shard_map/sd,hd->sh/dot_general | solution.py:23
  223.8 4.3 multiply_convert_fusion.7
  228.1 8.6 %convolution_convert_fusion.4 = bf16[512,2048]{1,0:T(8,128)(2,1)S(1)} fusion(bf16[2048,1,1536]{2,1,0:T(2,128)(2,1)} %get-tuple-element.18, bf16[512,768]{1,0:T(8,128)(2,1)} %get-tuple-element.24, bf16[512,768]{1,0:T(8,128)(2,1)} %get-tuple-element.23), kind=kOutput, calls=%fused_computation.27 | convolution fusion | flops 3225419776 | bytes 9961472 | tf_op jit(solution)/shard_map/sh,dh->sd/dot_general | solution.py:23
  236.8 3.9 convolution_convert_fusion.5
  240.8 3.3 fusion.10
  244.1 0.2 reduce-scatter.11.cloned.1.call-start
  244.3 1.3 copy-done.10
  245.7 6.8 %convolution_convert_fusion.1 = bf16[2048,1536]{1,0:T(8,128)(2,1)} fusion(bf16[512,2048]{1,0:T(8,128)(2,1)S(1)} %bitcast.95, bf16[512,768]{1,0:T(8,128)(2,1)} %get-tuple-element.22, bf16[512,768]{1,0:T(8,128)(2,1)} %get-tuple-element.21), kind=kOutput, calls=%fused_computation.1 | convolution fusion | flops 3227516928 | bytes 9961472 | tf_op jit(solution)/shard_map/sd,sh->dh/dot_general | solution.py:23
  252.5 0.0 reduce-scatter.13.cloned.1.call-start
  252.5 1.6 copy-done.8
  254.1 6.7 %convolution_convert_fusion = bf16[2048,1536]{1,0:T(8,128)(2,1)} fusion(bf16[512,2048]{1,0:T(8,128)(2,1)S(1)} %bitcast.93, bf16[512,768]{1,0:T(8,128)(2,1)} %get-tuple-element.24, bf16[512,768]{1,0:T(8,128)(2,1)} %get-tuple-element.23), kind=kOutput, calls=%fused_computation | convolution fusion | flops 3227516928 | bytes 9961472 | tf_op jit(solution)/shard_map/sd,sh->dh/dot_general | solution.py:23
  260.8 5.1 reduce-scatter.15.cloned.1.call-done
  266.0 62.6 %reduce-scatter.17.cloned.1.call-done = bf16[768,512]{1,0:T(8,128)(2,1)} async-done(((bf16[768,2048]{1,0:T(8,128)(2,1)}), bf16[768,512]{1,0:T(8,128)(2,1)}) %reduce-scatter.17.cloned.1.call-update) | async-done | bytes 786448 | tf_op jit(solution)/shard_map/reduce_scatter | solution.py:93
  328.6 1.6 pad_maximum_fusion.3
  330.1 2.8 copy.34
  332.9 55.9 %reduce-scatter.9.cloned.1.call-done = bf16[160,2048]{1,0:T(8,128)(2,1)} async-done(((bf16[1280,2048]{1,0:T(8,128)(2,1)}), bf16[160,2048]{1,0:T(8,128)(2,1)}) %reduce-scatter.9.cloned.1.call-update) | async-done | bytes 655376 | tf_op jit(solution)/shard_map/reduce_scatter | solution.py:63
  388.8 2.4 add_convert_fusion
  391.2 110.7 %reduce-scatter.11.cloned.1.call-done = bf16[512,1536]{1,0:T(8,128)(2,1)} async-done(((bf16[2048,1536]{1,0:T(8,128)(2,1)}), bf16[512,1536]{1,0:T(8,128)(2,1)}) %reduce-scatter.11.cloned.1.call-update) | async-done | bytes 1572880 | tf_op jit(solution)/shard_map/reduce_scatter | solution.py:95
  501.9 113.6 %reduce-scatter.13.cloned.1.call-done = bf16[512,1536]{1,0:T(8,128)(2,1)} async-done(((bf16[2048,1536]{1,0:T(8,128)(2,1)}), bf16[512,1536]{1,0:T(8,128)(2,1)}) %reduce-scatter.13.cloned.1.call-update) | async-done | bytes 1572880 | tf_op jit(solution)/shard_map/reduce_scatter | solution.py:95
  615.5 2.2 pad_maximum_fusion
  617.7 4.9 copy.33
  (85 shorter events, 0.5 us)
Async XLA Ops:
  7.2 59.5 %all-gather.9.cloned.1.call-start = ((), (), s32[]{:S(2)}) async-start(), calls=%async_computation.12 | async-start | bytes 5898240 | tf_op jit(solution)/shard_map/all_gather | solution.py:37
  7.9 144.8 %reduce-scatter.7.cloned.1.call-start = ((), (), s32[]{:S(2)}) async-start(), calls=%async_computation.6 | async-start | bytes 5898240 | tf_op jit(solution)/shard_map/reduce_scatter | solution.py:63
  30.6 16.8 %slice-start = ((s8[12582912]{0:T(1024)(128)(4,1)}), s8[4194304]{0:T(1024)(128)(4,1)S(1)}, s32[]{:S(2)}) async-start(s8[12582912]{0:T(1024)(128)(4,1)} %bitcast.70), calls=%async_computation.14 | async-start | bytes 8388608
  31.1 61.4 %copy-start.12 = (pred[8,64,160]{1,2,0:T(32,128)(4,1)}, pred[8,64,160]{1,2,0:T(32,128)(4,1)S(1)}, u32[]{:S(2)}) copy-start(pred[8,64,160]{1,2,0:T(32,128)(4,1)S(1)} %get-tuple-element.31) | copy-start | bytes 245764
  31.1 61.4 %copy-start.14 = (pred[8,64,160]{1,2,0:T(32,128)(4,1)}, pred[8,64,160]{1,2,0:T(32,128)(4,1)S(1)}, u32[]{:S(2)}) copy-start(pred[8,64,160]{1,2,0:T(32,128)(4,1)S(1)} %get-tuple-element.32) | copy-start | bytes 245764
  31.1 16.3 %slice-start.1 = ((s8[12582912]{0:T(1024)(128)(4,1)}), s8[4194304]{0:T(1024)(128)(4,1)S(1)}, s32[]{:S(2)}) async-start(s8[12582912]{0:T(1024)(128)(4,1)} %bitcast.70), calls=%async_computation.15 | async-start | bytes 8388608
  31.1 16.3 %slice-start.2 = ((s8[12582912]{0:T(1024)(128)(4,1)}), s8[4194304]{0:T(1024)(128)(4,1)S(1)}, s32[]{:S(2)}) async-start(s8[12582912]{0:T(1024)(128)(4,1)} %bitcast.70), calls=%async_computation.16 | async-start | bytes 8388608
  66.7 4.0 copy-start
  70.7 11.9 %copy-start.7 = (bf16[8,64,2048]{2,1,0:T(8,128)(2,1)}, bf16[8,64,2048]{2,1,0:T(8,128)(2,1)S(1)}, u32[]{:S(2)}) copy-start(bf16[8,64,2048]{2,1,0:T(8,128)(2,1)S(1)} %convolution_convert_fusion.6) | copy-start | bytes 6291460
  70.7 11.9 %slice-start.6 = ((s8[12582912]{0:T(1024)(128)(4,1)}), s8[4194304]{0:T(1024)(128)(4,1)S(1)}, s32[]{:S(2)}) async-start(s8[12582912]{0:T(1024)(128)(4,1)} %bitcast.80), calls=%async_computation.20 | async-start | bytes 8388608
  72.1 8.4 %copy-start.9 = (bf16[8,64,2048]{2,1,0:T(8,128)(2,1)}, bf16[8,64,2048]{2,1,0:T(8,128)(2,1)S(1)}, u32[]{:S(2)}) copy-start(bf16[8,64,2048]{2,1,0:T(8,128)(2,1)S(1)} %convolution_convert_fusion.7) | copy-start | bytes 6291460
  72.1 10.5 %slice-start.7 = ((s8[12582912]{0:T(1024)(128)(4,1)}), s8[4194304]{0:T(1024)(128)(4,1)S(1)}, s32[]{:S(2)}) async-start(s8[12582912]{0:T(1024)(128)(4,1)} %bitcast.80), calls=%async_computation.21 | async-start | bytes 8388608
  72.1 10.5 %slice-start.8 = ((s8[12582912]{0:T(1024)(128)(4,1)}), s8[4194304]{0:T(1024)(128)(4,1)S(1)}, s32[]{:S(2)}) async-start(s8[12582912]{0:T(1024)(128)(4,1)} %bitcast.80), calls=%async_computation.22 | async-start | bytes 8388608
  80.5 1.6 copy-start.2
  82.1 4.5 slice-start.9
  82.7 3.9 slice-start.10
  86.1 2.9 copy-start.4
  86.1 3.3 slice-start.13
  86.6 3.5 slice-start.14
  95.8 56.9 %copy-start.1 = (bf16[160,2048]{1,0:T(8,128)(2,1)S(1)}, bf16[160,2048]{1,0:T(8,128)(2,1)}, u32[]{:S(2)}) copy-start(bf16[160,2048]{1,0:T(8,128)(2,1)} %param.6) | copy-start | bytes 1966084
  95.8 56.9 %copy-start.5 = (bf16[160,2048]{1,0:T(8,128)(2,1)S(1)}, bf16[160,2048]{1,0:T(8,128)(2,1)}, u32[]{:S(2)}) copy-start(bf16[160,2048]{1,0:T(8,128)(2,1)} %param.7) | copy-start | bytes 1966084
  95.8 100.7 %all-gather.11.cloned.1.call-start = ((), (), s32[]{:S(2)}) async-start(), calls=%async_computation.13 | async-start | bytes 5898240 | tf_op jit(solution)/shard_map/all_gather | solution.py:83
  155.0 111.0 %reduce-scatter.15.cloned.1.call-start = ((), (), s32[]{:S(2)}) async-start(), calls=%async_computation.10 | async-start | bytes 3932160 | tf_op jit(solution)/shard_map/reduce_scatter | solution.py:93
  205.6 123.0 %reduce-scatter.17.cloned.1.call-start = ((), (), s32[]{:S(2)}) async-start(), calls=%async_computation.11 | async-start | bytes 3932160 | tf_op jit(solution)/shard_map/reduce_scatter | solution.py:93
  214.6 9.1 %slice-start.11 = ((s8[6291456]{0:T(1024)(128)(4,1)}), s8[2097152]{0:T(1024)(128)(4,1)S(1)}, s32[]{:S(2)}) async-start(s8[6291456]{0:T(1024)(128)(4,1)} %bitcast.84), calls=%async_computation.25 | async-start | bytes 4194304
  214.7 174.1 %reduce-scatter.9.cloned.1.call-start = ((), (), s32[]{:S(2)}) async-start(), calls=%async_computation.7 | async-start | bytes 5898240 | tf_op jit(solution)/shard_map/reduce_scatter | solution.py:63
  215.1 8.6 %slice-start.12 = ((s8[6291456]{0:T(1024)(128)(4,1)}), s8[4194304]{0:T(1024)(128)(4,1)S(1)}, s32[]{:S(2)}) async-start(s8[6291456]{0:T(1024)(128)(4,1)} %bitcast.84), calls=%async_computation.26 | async-start | bytes 8388608
  215.1 8.6 %copy-start.3 = (f32[512,1536]{1,0:T(8,128)S(1)}, f32[512,1536]{1,0:T(8,128)}, u32[]{:S(2)}) copy-start(f32[512,1536]{1,0:T(8,128)} %copy-done.2) | copy-start | bytes 9437188
  215.1 8.6 %copy-start.11 = (bf16[8,64,2048]{2,1,0:T(8,128)(2,1)S(1)}, bf16[8,64,2048]{2,1,0:T(8,128)(2,1)}, u32[]{:S(2)}) copy-start(bf16[8,64,2048]{2,1,0:T(8,128)(2,1)} %get-tuple-element.27) | copy-start | bytes 6291460
  223.7 13.0 %slice-start.3 = ((s8[12582912]{0:T(1024)(128)(4,1)}), s8[4194304]{0:T(1024)(128)(4,1)S(1)}, s32[]{:S(2)}) async-start(s8[12582912]{0:T(1024)(128)(4,1)} %bitcast.78), calls=%async_computation.17 | async-start | bytes 8388608
  223.7 13.0 %slice-start.4 = ((s8[12582912]{0:T(1024)(128)(4,1)}), s8[4194304]{0:T(1024)(128)(4,1)S(1)}, s32[]{:S(2)}) async-start(s8[12582912]{0:T(1024)(128)(4,1)} %bitcast.78), calls=%async_computation.18 | async-start | bytes 8388608
  228.1 8.7 %slice-start.5 = ((s8[12582912]{0:T(1024)(128)(4,1)}), s8[4194304]{0:T(1024)(128)(4,1)S(1)}, s32[]{:S(2)}) async-start(s8[12582912]{0:T(1024)(128)(4,1)} %bitcast.78), calls=%async_computation.19 | async-start | bytes 8388608
  228.1 8.7 %copy-start.16 = (bf16[512,768]{1,0:T(8,128)(2,1)S(1)}, bf16[512,768]{1,0:T(8,128)(2,1)}, u32[]{:S(2)}) copy-start(bf16[512,768]{1,0:T(8,128)(2,1)} %get-tuple-element.21) | copy-start | bytes 2359300
  228.1 8.7 %copy-start.17 = (bf16[512,768]{1,0:T(8,128)(2,1)S(1)}, bf16[512,768]{1,0:T(8,128)(2,1)}, u32[]{:S(2)}) copy-start(bf16[512,768]{1,0:T(8,128)(2,1)} %get-tuple-element.22) | copy-start | bytes 2359300
  236.8 3.9 copy-start.13
  236.8 3.9 copy-start.15
  244.1 1.6 copy-start.10
  244.1 257.8 %reduce-scatter.11.cloned.1.call-start = ((), (), s32[]{:S(2)}) async-start(), calls=%async_computation.8 | async-start | bytes 7864320 | tf_op jit(solution)/shard_map/reduce_scatter | solution.py:95
  252.4 1.6 copy-start.8
  252.5 363.0 %reduce-scatter.13.cloned.1.call-start = ((), (), s32[]{:S(2)}) async-start(), calls=%async_computation.9 | async-start | bytes 7864320 | tf_op jit(solution)/shard_map/reduce_scatter | solution.py:95
  328.6 60.2 %copy-start.6 = (bf16[160,2048]{1,0:T(8,128)(2,1)S(1)}, bf16[160,2048]{1,0:T(8,128)(2,1)}, u32[]{:S(2)}) copy-start(bf16[160,2048]{1,0:T(8,128)(2,1)} %reduce-scatter.7.cloned.1.call-done) | copy-start | bytes 1966084
Sparse Core Ops, SparseCore 0:
  9.9 43.8 all-gather.8
  95.9 56.7 reduce-scatter.6
  155.3 41.0 all-gather.10
  205.7 60.2 reduce-scatter.14
  268.2 60.2 reduce-scatter.16
  332.2 56.5 reduce-scatter.8
  391.1 110.7 reduce-scatter.10
  504.2 111.2 reduce-scatter.12
